TPU v7x, 256 devices: a whole 4x4x8 slice. The times are simulated.
256 devices in a mesh: fsdp: 16 (over z_lo, y), tp: 16 (over z_hi, x, core).
Axes of the slice: x: 4, y: 4, z: 8 (z_hi: 2, z_lo: 4; z = z_hi * 4 + z_lo), core: 2. Of those that a mesh axis runs over, the one named last changes fastest.
Arguments:
- output_gradient: bfloat16 [8192, 8192], P('fsdp'), may hold values from -6 to 6
- gate_pre: bfloat16 [8192, 14336], P('fsdp', 'tp'), may hold values from -6 to 6
- up_pre: bfloat16 [8192, 14336], P('fsdp', 'tp'), may hold values from -6 to 6
- down_weight: bfloat16 [14336, 8192], P('tp', 'fsdp'), may hold values from -0.046875 to 0.046875
- a_mean: float32 [8, 14336], P(None, 'tp'), may hold values from -0.75 to 0.75
- a_sigma: float32 [8, 14336], P(None, 'tp'), may hold values from 0.02 to 0.1
- a_noise: float32 [8, 14336], P(None, 'tp'), may hold values from -6 to 6
- second_factor: float32 [8, 8192], replicated, may hold values from -0.3125 to 0.3125
- in_signs: int32 [8192, 14336], P('fsdp', 'tp'), may hold values from -1 to 1, as said below
- out_signs: int32 [8192, 8], P('fsdp'), may hold values from -1 to 1, as said below
Outputs:
- d_gate: bfloat16 [8192, 14336], P('fsdp', 'tp')
- d_up: bfloat16 [8192, 14336], P('fsdp', 'tp')
- d_mean: float32 [8, 14336], P(None, 'tp')
- d_sigma: float32 [8, 14336], P(None, 'tp')
- second_factor_gradient: float32 [8, 8192], P(None, 'tp')
Inputs may be any that keep to these rules, and one draw needn't show every extreme that they name: `in_signs`: every entry is -1 or +1. `out_signs`: every entry is -1 or +1.
All inputs are finite; a program needn't handle non-finite values.
Results may differ from a plain program's by a relative error of at most 0.0031.
Values may be sent and summed in bfloat16 or wider, within the bound.
A program may use at most 128 MiB of HBM per device.

v0:
```python
import math
import jax
import jax.numpy as jnp
from jax import lax
from jax.sharding import PartitionSpec as P

adapter_scale = 2.0


def contract_last(left_rows, right_rows):
    return lax.dot_general(
        left_rows, right_rows, (((1,), (1,)), ((), ())), preferred_element_type=jnp.float32
    )


def local(
    output_gradient,
    gate_pre,
    up_pre,
    down_weight,
    a_mean,
    a_sigma,
    a_noise,
    second_factor,
    in_signs,
    out_signs,
):
    highest_precision = lax.Precision.HIGHEST
    gate_wide = gate_pre.astype(jnp.float32)
    up_wide = up_pre.astype(jnp.float32)
    sigmoid_gate = jax.nn.sigmoid(gate_wide)
    hidden = (gate_wide * sigmoid_gate * up_wide).astype(jnp.bfloat16)
    spread = a_sigma * a_noise
    sign_in = in_signs.astype(jnp.float32)
    sign_out = out_signs.astype(jnp.float32)
    flipped = hidden * sign_in
    rank_local = jnp.dot(
        hidden, a_mean.T, precision=highest_precision, preferred_element_type=jnp.float32
    ) + sign_out * jnp.dot(
        flipped, spread.T, precision=highest_precision, preferred_element_type=jnp.float32
    )
    rank_values = lax.psum(rank_local, "tp")
    rank_gradient = adapter_scale * jnp.dot(
        output_gradient,
        second_factor.T,
        precision=highest_precision,
        preferred_element_type=jnp.float32,
    )
    tok_count = output_gradient.shape[0]
    base_grad = contract_last(
        output_gradient, lax.all_gather(down_weight, "fsdp", axis=1, tiled=True)
    )
    signed_grad = rank_gradient * sign_out
    hidden_grad = (
        base_grad
        + jnp.dot(
            rank_gradient, a_mean, precision=highest_precision, preferred_element_type=jnp.float32
        )
        + sign_in
        * jnp.dot(
            signed_grad, spread, precision=highest_precision, preferred_element_type=jnp.float32
        )
    )
    d_gate = (
        hidden_grad * up_wide * sigmoid_gate * (1.0 + gate_wide * (1.0 - sigmoid_gate))
    ).astype(jnp.bfloat16)
    d_up = (hidden_grad * gate_wide * sigmoid_gate).astype(jnp.bfloat16)
    out_width = output_gradient.shape[1] // lax.axis_size("tp")
    out_cols = lax.dynamic_slice_in_dim(
        output_gradient, lax.axis_index("tp") * out_width, out_width, 1
    )
    mean_part = jnp.dot(
        rank_gradient.T, hidden, precision=highest_precision, preferred_element_type=jnp.float32
    )
    sigma_part = jnp.dot(
        signed_grad.T, flipped, precision=highest_precision, preferred_element_type=jnp.float32
    )
    factor_part = jnp.dot(
        rank_values.T, out_cols, precision=highest_precision, preferred_element_type=jnp.float32
    )
    mean_sum, sigma_sum, factor_total = lax.psum((mean_part, sigma_part, factor_part), "fsdp")
    normalizing_count = 1.0 / math.sqrt(tok_count * lax.axis_size("fsdp"))
    d_mean = normalizing_count * mean_sum
    d_sigma = normalizing_count * a_noise * sigma_sum
    second_factor_gradient = normalizing_count * adapter_scale * factor_total
    return (d_gate, d_up, d_mean, d_sigma, second_factor_gradient)


def solution(mesh):
    placed = (
        P("fsdp", None),
        P("fsdp", "tp"),
        P("fsdp", "tp"),
        P("tp", "fsdp"),
        P(None, "tp"),
        P(None, "tp"),
        P(None, "tp"),
        P(),
        P("fsdp", "tp"),
        P("fsdp", None),
    )
    return jax.shard_map(
        local,
        mesh=mesh,
        in_specs=placed,
        out_specs=(P("fsdp", "tp"), P("fsdp", "tp"), P(None, "tp"), P(None, "tp"), P(None, "tp")),
        check_vma=False,
    )
```

profile of v0, /device:TPU:8, one launch (start us, length us, event | category | flops | bytes accessed | tf_op | source)
XLA Modules:
  0.0 444.5 jit_solution(13460722747519460938)
XLA Ops:
  7.2 0.0 copy-start
  7.2 0.0 all-gather.2.cloned.1.call-start
  7.2 0.7 all-gather.2.cloned.1.call-update
  7.9 0.0 all-reduce.3.cloned.1.call-start
  8.0 0.2 copy-done
  8.1 0.0 copy-start.5
  8.1 0.0 copy-start.4
  8.1 8.9 %convolution_multiply_fusion = f32[512,8]{0,1:T(8,128)S(1)} fusion(bf16[512,8192]{1,0:T(8,128)(2,1)} %param.10, f32[8,8192]{1,0:T(8,128)S(1)} %copy-done), kind=kOutput, calls=%fused_computation.22 | convolution fusion | flops 402657280 | bytes 8667136 | tf_op jit(solution)/shard_map/dot_general | solution.py:43
  17.1 0.0 copy-done.5
  17.1 0.0 copy-start.2
  17.1 0.0 copy-start.3
  17.1 0.0 copy-start.1
  17.1 2.9 fusion.20
  20.0 0.0 copy-done.4
  20.0 0.0 copy-done.2
  20.0 0.0 copy-done.3
  20.0 2.9 fusion.17
  22.9 151.3 %all-gather.2.cloned.1.call-done = bf16[896,8192]{1,0:T(8,128)(2,1)} async-done(((bf16[896,512]{1,0:T(8,128)(2,1)}), bf16[896,8192]{1,0:T(8,128)(2,1)}) %all-gather.2.cloned.1.call-update) | async-done | bytes 14680080 | tf_op jit(solution)/shard_map/all_gather | solution.py:51
  174.2 0.0 copy-done.1
  174.2 18.6 %fusion.9 = (bf16[512,896]{1,0:T(8,128)(2,1)}, bf16[512,896]{1,0:T(8,128)(2,1)}, bf16[512,896]{1,0:T(8,128)(2,1)S(1)}) fusion(bf16[512,896]{1,0:T(8,128)(2,1)} %param.11, bf16[512,896]{1,0:T(8,128)(2,1)} %param.12, f32[512,896]{1,0:T(8,128)} %fusion.17, s32[512,896]{1,0:T(8,128)S(1)} %copy-done.1, f32[512,896]{1,0:T(8,128)} %fusion.20, ...), kind=kOutput, calls=%fused_computation.15 | convolution fusion | flops 7526285312 | bytes 33161216 | tf_op jit(solution)/shard_map/dot_general | solution.py:11
  192.8 0.8 fusion.22
  193.6 1.8 fusion.11
  195.3 1.1 fusion.21
  196.4 1.8 fusion.13
  198.2 91.3 %psum.30 = f32[512,8]{0,1:T(8,128)S(1)} all-reduce(f32[512,8]{0,1:T(8,128)S(1)} %fusion.13), channel_id=1, replica_groups=mesh['fsdp'=16,'tp'=16] {'tp'}, use_global_device_ids=true, to_apply=%region_2.0 | all-reduce | flops 4096 | bytes 32768 | tf_op jit(solution)/shard_map/psum | solution.py:42
  289.5 2.0 fusion.14
  291.5 0.0 all-reduce.3.cloned.1.call-update
  291.5 143.5 %all-reduce.3.cloned.1.call-done = (f32[8,896]{1,0:T(8,128)}, f32[8,896]{1,0:T(8,128)}, f32[8,512]{1,0:T(8,128)}) async-done(((f32[8,896]{1,0:T(8,128)}, f32[8,896]{1,0:T(8,128)}, f32[8,512]{1,0:T(8,128)}), (f32[8,896]{1,0:T(8,128)}, f32[8,896]{1,0:T(8,128)}, f32[8,512]{1,0:T(8,128)})) %all-reduce.3.cloned.1.call-update) | async-done | bytes 73744 | tf_op jit(solution)/shard_map/psum | solution.py:81
  435.0 1.3 broadcast_multiply_fusion.1
  436.3 1.4 multiply_multiply_fusion
Async XLA Ops:
  7.2 1.0 copy-start
  7.2 167.0 %all-gather.2.cloned.1.call-start = ((), (), s32[]{:S(2)}) async-start(), calls=%async_computation | async-start | bytes 15597568 | tf_op jit(solution)/shard_map/all_gather | solution.py:51
  7.9 427.1 %all-reduce.3.cloned.1.call-start = ((), (), s32[]{:S(2)}) async-start(), calls=%async_computation.1 | async-start | bytes 147456 | tf_op jit(solution)/shard_map/psum | solution.py:81
  8.1 8.9 %copy-start.5 = (f32[8,896]{1,0:T(8,128)S(1)}, f32[8,896]{1,0:T(8,128)}, u32[]{:S(2)}) copy-start(f32[8,896]{1,0:T(8,128)} %param.14) | copy-start | bytes 86020
  8.1 11.9 %copy-start.4 = (f32[8,896]{1,0:T(8,128)S(1)}, f32[8,896]{1,0:T(8,128)}, u32[]{:S(2)}) copy-start(f32[8,896]{1,0:T(8,128)} %param.15) | copy-start | bytes 86020
  17.1 2.9 copy-start.2
  17.1 2.9 copy-start.3
  17.1 157.1 %copy-start.1 = (s32[512,896]{1,0:T(8,128)S(1)}, s32[512,896]{1,0:T(8,128)}, u32[]{:S(2)}) copy-start(s32[512,896]{1,0:T(8,128)} %param.18) | copy-start | bytes 5505028
Sparse Core Ops, SparseCore 0:
  9.8 164.3 all-gather.1
  291.6 143.2 all-reduce.2
where the time goes:
time: 445 us
  waiting for transfers between devices  295 us (66%)
  blocking collectives  91.3 us (21%)
  matrix products  40.7 us (9%)
  between operations  14.1 us (3%)
    all_gather x1, waiting for transfers between devices, local(): lax.all_gather(down_weight, 'fsdp', axis=1, tiled=True)  151 us
    psum x1, waiting for transfers between devices, local(): lax.psum((mean_part, sigma_part, factor_part), 'fsdp')  143 us
    psum x1, blocking collectives, local(): rank_values = lax.psum(rank_local, 'tp')  91.3 us
    dot_general x1, matrix products, contract_last(): lax.dot_general(left_rows, right_rows, (((1,), (1,)), ((), ())), preferre...  18.6 us
    dot_general x1, matrix products, local(): jnp.dot(output_gradient, second_factor.T, precision=highest_precision, pr...  8.92 us
  transfers between devices with their start and end apart: 2, of which 2 were waited for; matrix products, arithmetic and copies ran while one was open for 3% of the time, Pallas kernels for 0%

commit v1 on v0

--- a/solution.py
+++ b/solution.py
@@ -48,7 +48,10 @@
     )
     tok_count = output_gradient.shape[0]
     base_grad = contract_last(
-        output_gradient, lax.all_gather(down_weight, "fsdp", axis=1, tiled=True)
+        output_gradient,
+        jnp.concatenate(
+            lax.all_to_all(jnp.stack([down_weight] * lax.axis_size("fsdp")), "fsdp", 0, 0), axis=1
+        ),
     )
     signed_grad = rank_gradient * sign_out
     hidden_grad = (

time: 445 us -> 610 us (1.37)
  waiting for transfers between devices: 295 us -> 446 us
  starting transfers between devices: 0.08 us -> 9.03 us
  local copies, waits for them, and re-layouts: 0.19 us -> 8.81 us
    all_to_all x0 -> x1, waiting for transfers between devices: none -> 246 us  [local(): lax.all_to_all(jnp.stack([down_weight] * lax.axis_size('fsdp')), 'fsdp',...]
    all_gather x1 -> x0, waiting for transfers between devices: 151 us -> none  [local(): lax.all_gather(down_weight, 'fsdp', axis=1, tiled=True)]
    psum x1, waiting for transfers between devices: 143 us -> 200 us  [local(): lax.psum((mean_part, sigma_part, factor_part), 'fsdp')]
    all_to_all x0 -> x1, starting transfers between devices: none -> 8.99 us  [local(): lax.all_to_all(jnp.stack([down_weight] * lax.axis_size('fsdp')), 'fsdp',...]
    another operation x0 -> x1, local copies, waits for them, and re-layouts: none -> 7.18 us  [local(): jnp.stack([down_weight] * lax.axis_size('fsdp'))]
  transfers between devices with their start and end apart: 2 -> 2, of which waited for: 2 -> 2; matrix products, arithmetic and copies ran while one was open for 3% -> 2% of each run, Pallas kernels for 0% -> 0%
where the time goes in v1:
time: 610 us
  waiting for transfers between devices  446 us (73%)
  blocking collectives  88.8 us (15%)
  matrix products  40.2 us (7%)
  between operations  14.1 us (2%)
  starting transfers between devices  9.03 us (1%)
  local copies, waits for them, and re-layouts  8.81 us (1%)
    all_to_all x1, waiting for transfers between devices, local(): lax.all_to_all(jnp.stack([down_weight] * lax.axis_size('fsdp')), 'fsdp',...  246 us
    psum x1, waiting for transfers between devices, local(): lax.psum((mean_part, sigma_part, factor_part), 'fsdp')  200 us
    psum x1, blocking collectives, local(): rank_values = lax.psum(rank_local, 'tp')  88.8 us
    dot_general x1, matrix products, contract_last(): lax.dot_general(left_rows, right_rows, (((1,), (1,)), ((), ())), preferre...  18 us
  transfers between devices with their start and end apart: 2, of which 2 were waited for; matrix products, arithmetic and copies ran while one was open for 2% of the time, Pallas kernels for 0%

profile of v1, /device:TPU:8, one launch (start us, length us, event | category | flops | bytes accessed | tf_op | source)
XLA Modules:
  0.0 609.7 jit_solution(11583021310519142386)
XLA Ops:
  7.2 0.0 copy-start
  7.2 1.6 copy.15
  8.8 7.2 %stack.2 = bf16[16,896,512]{1,2,0:T(8,128)(2,1)} broadcast(bf16[896,512]{0,1:T(8,128)(2,1)S(1)} %copy.15), dimensions={1,2} | broadcast | bytes 15597568 | tf_op jit(solution)/shard_map/stack | solution.py:53
  15.9 9.0 %all-to-all-start = ((bf16[16,896,512]{1,2,0:T(8,128)(2,1)}), bf16[16,896,512]{1,2,0:T(8,128)(2,1)}, u32[]{:S(2)}, u32[]{:S(2)}) async-start(bf16[16,896,512]{1,2,0:T(8,128)(2,1)} %stack.2), calls=%async_computation | async-start | bytes 29360128 | tf_op jit(solution)/shard_map/all_to_all | solution.py:53
  24.9 0.0 all-reduce.3.cloned.1.call-start
  25.0 0.0 copy-done
  25.0 0.0 copy-start.5
  25.0 0.0 copy-start.4
  25.0 8.9 %convolution_multiply_fusion = f32[512,8]{0,1:T(8,128)S(1)} fusion(bf16[512,8192]{1,0:T(8,128)(2,1)} %param.10, f32[8,8192]{1,0:T(8,128)S(1)} %copy-done), kind=kOutput, calls=%fused_computation.22 | convolution fusion | flops 402657280 | bytes 8667136 | tf_op jit(solution)/shard_map/dot_general | solution.py:43
  34.0 0.0 copy-done.5
  34.0 0.0 copy-start.2
  34.0 0.0 copy-start.3
  34.0 0.0 copy-start.1
  34.0 0.0 copy-start.6
  34.0 2.9 fusion.20
  36.9 0.0 copy-done.4
  36.9 0.0 copy-done.2
  36.9 0.0 copy-done.3
  36.9 2.9 fusion.17
  39.8 246.2 %all-to-all-done = bf16[16,896,512]{1,2,0:T(8,128)(2,1)} async-done(((bf16[16,896,512]{1,2,0:T(8,128)(2,1)}), bf16[16,896,512]{1,2,0:T(8,128)(2,1)}, u32[]{:S(2)}, u32[]{:S(2)}) %all-to-all-start) | async-done | bytes 14680096 | tf_op jit(solution)/shard_map/all_to_all | solution.py:53
  286.0 0.0 copy-done.1
  286.0 0.0 copy-done.6
  286.0 18.0 %fusion.9 = (bf16[512,896]{1,0:T(8,128)(2,1)}, bf16[512,896]{1,0:T(8,128)(2,1)}, bf16[512,896]{1,0:T(8,128)(2,1)S(1)}) fusion(bf16[512,896]{1,0:T(8,128)(2,1)S(1)} %copy-done.6, bf16[512,896]{1,0:T(8,128)(2,1)} %param.12, f32[512,896]{1,0:T(8,128)} %fusion.17, s32[512,896]{1,0:T(8,128)S(1)} %copy-done.1, f32[512,896]{1,0:T(8,128)} %fusion.20, ...), kind=kOutput, calls=%fused_computation.15 | convolution fusion | flops 7526285312 | bytes 33161216 | tf_op jit(solution)/shard_map/dot_general | solution.py:11
  304.1 0.8 fusion.22
  304.9 1.8 fusion.11
  306.6 1.1 fusion.21
  307.7 1.8 fusion.13
  309.5 88.8 %psum.30 = f32[512,8]{0,1:T(8,128)S(1)} all-reduce(f32[512,8]{0,1:T(8,128)S(1)} %fusion.13), channel_id=1, replica_groups=mesh['fsdp'=16,'tp'=16] {'tp'}, use_global_device_ids=true, to_apply=%region_2.0 | all-reduce | flops 4096 | bytes 32768 | tf_op jit(solution)/shard_map/psum | solution.py:42
  398.3 2.0 fusion.14
  400.3 0.0 all-reduce.3.cloned.1.call-update
  400.3 199.8 %all-reduce.3.cloned.1.call-done = (f32[8,896]{1,0:T(8,128)}, f32[8,896]{1,0:T(8,128)}, f32[8,512]{1,0:T(8,128)}) async-done(((f32[8,896]{1,0:T(8,128)}, f32[8,896]{1,0:T(8,128)}, f32[8,512]{1,0:T(8,128)}), (f32[8,896]{1,0:T(8,128)}, f32[8,896]{1,0:T(8,128)}, f32[8,512]{1,0:T(8,128)})) %all-reduce.3.cloned.1.call-update) | async-done | bytes 73744 | tf_op jit(solution)/shard_map/psum | solution.py:84
  600.1 1.3 broadcast_multiply_fusion.1
  601.4 1.4 multiply_multiply_fusion
Async XLA Ops:
  7.2 17.8 %copy-start = (f32[8,8192]{1,0:T(8,128)S(1)}, f32[8,8192]{1,0:T(8,128)}, u32[]{:S(2)}) copy-start(f32[8,8192]{1,0:T(8,128)} %param.17) | copy-start | bytes 786436
  15.9 270.1 %all-to-all-start = ((bf16[16,896,512]{1,2,0:T(8,128)(2,1)}), bf16[16,896,512]{1,2,0:T(8,128)(2,1)}, u32[]{:S(2)}, u32[]{:S(2)}) async-start(bf16[16,896,512]{1,2,0:T(8,128)(2,1)} %stack.2), calls=%async_computation | async-start | bytes 29360128 | tf_op jit(solution)/shard_map/all_to_all | solution.py:53
  24.9 575.2 %all-reduce.3.cloned.1.call-start = ((), (), s32[]{:S(2)}) async-start(), calls=%async_computation.1 | async-start | bytes 147456 | tf_op jit(solution)/shard_map/psum | solution.py:84
  25.0 9.0 %copy-start.5 = (f32[8,896]{1,0:T(8,128)S(1)}, f32[8,896]{1,0:T(8,128)}, u32[]{:S(2)}) copy-start(f32[8,896]{1,0:T(8,128)} %param.14) | copy-start | bytes 86020
  25.0 11.9 %copy-start.4 = (f32[8,896]{1,0:T(8,128)S(1)}, f32[8,896]{1,0:T(8,128)}, u32[]{:S(2)}) copy-start(f32[8,896]{1,0:T(8,128)} %param.15) | copy-start | bytes 86020
  34.0 2.9 copy-start.2
  34.0 2.9 copy-start.3
  34.0 252.0 %copy-start.1 = (s32[512,896]{1,0:T(8,128)S(1)}, s32[512,896]{1,0:T(8,128)}, u32[]{:S(2)}) copy-start(s32[512,896]{1,0:T(8,128)} %param.18) | copy-start | bytes 5505028
  34.0 252.0 %copy-start.6 = (bf16[512,896]{1,0:T(8,128)(2,1)S(1)}, bf16[512,896]{1,0:T(8,128)(2,1)}, u32[]{:S(2)}) copy-start(bf16[512,896]{1,0:T(8,128)(2,1)} %param.11) | copy-start | bytes 2752516
Sparse Core Ops, SparseCore 0:
  400.5 199.6 all-reduce.2

commit v2 on v0

--- a/solution.py
+++ b/solution.py
@@ -39,7 +39,7 @@
     ) + sign_out * jnp.dot(
         flipped, spread.T, precision=highest_precision, preferred_element_type=jnp.float32
     )
-    rank_values = lax.psum(rank_local, "tp")
+    rank_values = jnp.sum(lax.all_gather(rank_local, "tp"), axis=0)
     rank_gradient = adapter_scale * jnp.dot(
         output_gradient,
         second_factor.T,

time: 445 us -> 386 us (0.87)
  blocking collectives: 91.3 us -> 32.3 us
    psum x1 -> x0, blocking collectives: 91.3 us -> none  [local(): rank_values = lax.psum(rank_local, 'tp')]
    all_gather x0 -> x1, blocking collectives: none -> 32.3 us  [local(): rank_values = jnp.sum(lax.all_gather(rank_local, 'tp'), axis=0)]
  transfers between devices with their start and end apart: 2 -> 2, of which waited for: 2 -> 2; matrix products, arithmetic and copies ran while one was open for 3% -> 4% of each run, Pallas kernels for 0% -> 0%
where the time goes in v2:
time: 386 us
  waiting for transfers between devices  295 us (76%)
  matrix products  40.7 us (11%)
  blocking collectives  32.3 us (8%)
  between operations  14.1 us (4%)
    all_gather x1, waiting for transfers between devices, local(): lax.all_gather(down_weight, 'fsdp', axis=1, tiled=True)  151 us
    psum x1, waiting for transfers between devices, local(): lax.psum((mean_part, sigma_part, factor_part), 'fsdp')  143 us
    all_gather x1, blocking collectives, local(): rank_values = jnp.sum(lax.all_gather(rank_local, 'tp'), axis=0)  32.3 us
    dot_general x1, matrix products, contract_last(): lax.dot_general(left_rows, right_rows, (((1,), (1,)), ((), ())), preferre...  18.6 us
    dot_general x1, matrix products, local(): jnp.dot(output_gradient, second_factor.T, precision=highest_precision, pr...  8.92 us
  transfers between devices with their start and end apart: 2, of which 2 were waited for; matrix products, arithmetic and copies ran while one was open for 4% of the time, Pallas kernels for 0%

profile of v2, /device:TPU:8, one launch (start us, length us, event | category | flops | bytes accessed | tf_op | source)
XLA Modules:
  0.0 385.6 jit_solution(9758014767961971174)
XLA Ops:
  7.2 0.0 copy-start
  7.2 0.0 all-gather.3.cloned.1.call-start
  7.2 0.7 all-gather.3.cloned.1.call-update
  7.9 0.0 all-reduce.3.cloned.1.call-start
  8.0 0.2 copy-done
  8.1 0.0 copy-start.5
  8.1 0.0 copy-start.4
  8.1 8.9 %convolution_multiply_fusion = f32[512,8]{0,1:T(8,128)S(1)} fusion(bf16[512,8192]{1,0:T(8,128)(2,1)} %param.10, f32[8,8192]{1,0:T(8,128)S(1)} %copy-done), kind=kOutput, calls=%fused_computation.22 | convolution fusion | flops 402657280 | bytes 8667136 | tf_op jit(solution)/shard_map/dot_general | solution.py:43
  17.1 0.0 copy-done.5
  17.1 0.0 copy-start.2
  17.1 0.0 copy-start.3
  17.1 0.0 copy-start.1
  17.1 2.9 fusion.20
  20.0 0.0 copy-done.4
  20.0 0.0 copy-done.2
  20.0 0.0 copy-done.3
  20.0 2.9 fusion.17
  22.9 151.3 %all-gather.3.cloned.1.call-done = bf16[896,8192]{1,0:T(8,128)(2,1)} async-done(((bf16[896,512]{1,0:T(8,128)(2,1)}), bf16[896,8192]{1,0:T(8,128)(2,1)}) %all-gather.3.cloned.1.call-update) | async-done | bytes 14680080 | tf_op jit(solution)/shard_map/all_gather | solution.py:51
  174.2 0.0 copy-done.1
  174.2 18.6 %fusion.9 = (bf16[512,896]{1,0:T(8,128)(2,1)}, bf16[512,896]{1,0:T(8,128)(2,1)}, bf16[512,896]{1,0:T(8,128)(2,1)S(1)}) fusion(bf16[512,896]{1,0:T(8,128)(2,1)} %param.11, bf16[512,896]{1,0:T(8,128)(2,1)} %param.12, f32[512,896]{1,0:T(8,128)} %fusion.17, s32[512,896]{1,0:T(8,128)S(1)} %copy-done.1, f32[512,896]{1,0:T(8,128)} %fusion.20, ...), kind=kOutput, calls=%fused_computation.15 | convolution fusion | flops 7526285312 | bytes 33161216 | tf_op jit(solution)/shard_map/dot_general | solution.py:11
  192.8 0.8 fusion.22
  193.6 1.8 fusion.11
  195.3 1.1 fusion.21
  196.4 1.8 fusion.13
  198.2 32.3 %all-gather = f32[8192,8]{0,1:T(8,128)S(1)} all-gather(f32[512,8]{0,1:T(8,128)S(1)} %fusion.13), channel_id=2, replica_groups=mesh['fsdp'=16,'tp'=16] {'tp'}, dimensions={0}, use_global_device_ids=true | all-gather | bytes 278528 | tf_op jit(solution)/shard_map/all_gather | solution.py:42
  230.6 2.0 fusion.14
  232.5 0.0 all-reduce.3.cloned.1.call-update
  232.6 143.4 %all-reduce.3.cloned.1.call-done = (f32[8,896]{1,0:T(8,128)}, f32[8,896]{1,0:T(8,128)}, f32[8,512]{1,0:T(8,128)}) async-done(((f32[8,896]{1,0:T(8,128)}, f32[8,896]{1,0:T(8,128)}, f32[8,512]{1,0:T(8,128)}), (f32[8,896]{1,0:T(8,128)}, f32[8,896]{1,0:T(8,128)}, f32[8,512]{1,0:T(8,128)})) %all-reduce.3.cloned.1.call-update) | async-done | bytes 73744 | tf_op jit(solution)/shard_map/psum | solution.py:81
  376.0 1.3 broadcast_multiply_fusion.1
  377.3 1.4 multiply_multiply_fusion
  (1 shorter events, 0.0 us)
Async XLA Ops:
  7.2 1.0 copy-start
  7.2 167.0 %all-gather.3.cloned.1.call-start = ((), (), s32[]{:S(2)}) async-start(), calls=%async_computation | async-start | bytes 15597568 | tf_op jit(solution)/shard_map/all_gather | solution.py:51
  7.9 368.1 %all-reduce.3.cloned.1.call-start = ((), (), s32[]{:S(2)}) async-start(), calls=%async_computation.1 | async-start | bytes 147456 | tf_op jit(solution)/shard_map/psum | solution.py:81
  8.1 8.9 %copy-start.5 = (f32[8,896]{1,0:T(8,128)S(1)}, f32[8,896]{1,0:T(8,128)}, u32[]{:S(2)}) copy-start(f32[8,896]{1,0:T(8,128)} %param.14) | copy-start | bytes 86020
  8.1 11.9 %copy-start.4 = (f32[8,896]{1,0:T(8,128)S(1)}, f32[8,896]{1,0:T(8,128)}, u32[]{:S(2)}) copy-start(f32[8,896]{1,0:T(8,128)} %param.15) | copy-start | bytes 86020
  17.1 2.9 copy-start.2
  17.1 2.9 copy-start.3
  17.1 157.1 %copy-start.1 = (s32[512,896]{1,0:T(8,128)S(1)}, s32[512,896]{1,0:T(8,128)}, u32[]{:S(2)}) copy-start(s32[512,896]{1,0:T(8,128)} %param.18) | copy-start | bytes 5505028
Sparse Core Ops, SparseCore 0:
  9.8 164.3 all-gather.2
  232.7 143.2 all-reduce.2
